TPU v7x, 256 devices: a whole 4x4x8 slice. The times are simulated.
256 devices in a mesh: fsdp: 64 (over x, z, y_lo), tile: 4 (over y_hi, core).
Axes of the slice: x: 4, y: 4 (y_hi: 2, y_lo: 2; y = y_hi * 2 + y_lo), z: 8, core: 2. Of those that a mesh axis runs over, the one named last changes fastest.
Arguments:
- tokens: bfloat16 [65536, 1536], P('fsdp', 'tile'), may hold values from -6 to 6
- ln_gain: float32 [1536], replicated, may hold values from 0.25 to 1.75
- w_up: bfloat16 [1536, 6144], P('fsdp', 'tile'), may hold values from -0.15625 to 0.15625
- w_down: bfloat16 [6144, 1536], P('tile', 'fsdp'), may hold values from -0.078125 to 0.078125
- w_flux_in: bfloat16 [1536, 768], P('tile'), may hold values from -0.15625 to 0.15625
- w_flux_out: bfloat16 [768, 128], replicated, may hold values from -0.21875 to 0.21875
- ocean_state: bfloat16 [2048, 128, 256], P('fsdp', 'tile'), may hold values from -6 to 6
- land_mask: int32 [2048, 128], P('fsdp', 'tile'), may hold values from 0 to 1, as said below
- column_map: int32 [2048, 128], P('fsdp', 'tile'), may hold values from 0 to 65535, as said below
- w_couple: bfloat16 [128, 256], replicated, may hold values from -0.5 to 0.5
- dw_kernel: float32 [2, 7, 7, 256], replicated, may hold values from -0.875 to 0.875
- ocean_gain: float32 [2, 256], replicated, may hold values from 0.25 to 1.75
- w_pw1: bfloat16 [2, 256, 1024], replicated, may hold values from -0.375 to 0.375
- w_pw2: bfloat16 [2, 1024, 256], replicated, may hold values from -0.1875 to 0.1875
Outputs:
- atm_out: bfloat16 [65536, 1536], P('fsdp', 'tile')
- ocean_out: bfloat16 [2048, 128, 256], P('fsdp', 'tile')
Inputs may be any that keep to these rules, and one draw needn't show every extreme that they name: `land_mask`: 0 or 1; land comes in regions of 8 x 8 cells whose ocean share varies. `column_map`: the column in grid row x names a token between (x // 32) * 1024 - 256 and (x // 32 + 1) * 1024 + 255.
All inputs are finite; a program needn't handle non-finite values.
Results may differ from a plain program's by a relative error of at most 0.014.
Values may be sent and summed in bfloat16 or wider, within the bound.
A program may use at most 128 MiB of HBM per device.

v0:
```python
import jax
import jax.numpy as jnp
from jax import lax
from jax.sharding import PartitionSpec as P


def with_halo(block, sides, width):
    for axis, dim in sides:
        count = lax.axis_size(axis)
        forward = [(i, i + 1) for i in range(count - 1)]
        backward = [(target, source) for source, target in forward]
        low = lax.ppermute(
            lax.slice_in_dim(block, block.shape[dim] - width, None, axis=dim), axis, forward
        )
        high = lax.ppermute(lax.slice_in_dim(block, 0, width, axis=dim), axis, backward)
        block = jnp.concatenate([low, block, high], axis=dim)
    return block


def layer_norm(values, gain):
    center = values - jnp.mean(values, axis=-1, keepdims=True)
    spread = jnp.mean(center * center, axis=-1, keepdims=True)
    return center * lax.rsqrt(spread + 1e-06) * gain


def conv_block(padded, region_mask, kernel, gain, w_one, w_two):
    rows = padded.shape[0] - 6
    cols = padded.shape[1] - 6
    chans = padded.shape[2]
    total = jnp.zeros((rows, cols, chans), jnp.float32)
    for first in range(7):
        for second in range(7):
            total = (
                total
                + padded[first : first + rows, second : second + cols].astype(jnp.float32)
                * kernel[first, second]
            )
    pnorm = layer_norm(total, gain).astype(jnp.bfloat16).reshape(rows * cols, chans)
    inner = jax.nn.gelu(
        jnp.dot(pnorm, w_one, preferred_element_type=jnp.float32), approximate=True
    ).astype(jnp.bfloat16)
    lowered = jnp.dot(inner, w_two, preferred_element_type=jnp.float32).reshape(rows, cols, chans)
    before = padded[3 : 3 + rows, 3 : 3 + cols].astype(jnp.float32)
    return (region_mask[..., None] * (before + lowered)).astype(jnp.bfloat16)


def body(
    tokens,
    ln_gain,
    w_up,
    w_down,
    w_flux_in,
    w_flux_out,
    ocean_state,
    land_mask,
    column_map,
    w_couple,
    dw_kernel,
    ocean_gain,
    w_pw1,
    w_pw2,
):
    band_rows = tokens.shape[0]
    whole = lax.all_gather(tokens, "tile", axis=1, tiled=True)
    normed = layer_norm(whole.astype(jnp.float32), ln_gain).astype(jnp.bfloat16)
    up_whole = lax.all_gather(w_up, "fsdp", axis=0, tiled=True)
    pre = jnp.dot(normed, up_whole, preferred_element_type=jnp.float32)
    hidden = jax.nn.gelu(pre, approximate=True).astype(jnp.bfloat16)
    down_whole = lax.all_gather(w_down, "fsdp", axis=1, tiled=True)
    terms = jnp.dot(hidden, down_whole, preferred_element_type=jnp.float32)
    delta = lax.psum_scatter(terms, "tile", scatter_dimension=1, tiled=True)
    atm_out = (tokens.astype(jnp.float32) + delta).astype(jnp.bfloat16)
    flux_pre = lax.psum(jnp.dot(atm_out, w_flux_in, preferred_element_type=jnp.float32), "tile")
    flux_hidden = jax.nn.gelu(flux_pre, approximate=True).astype(jnp.bfloat16)
    fluxes = jnp.dot(flux_hidden, w_flux_out, preferred_element_type=jnp.float32).astype(
        jnp.bfloat16
    )
    rim_rows = band_rows // 4
    window = with_halo(fluxes, (("fsdp", 0),), rim_rows)
    band = lax.axis_index("fsdp")
    local_index = (column_map - (band * band_rows - rim_rows)).reshape(-1)
    picked = jnp.take(window, local_index, axis=0)
    grid_rows = ocean_state.shape[0]
    grid_cols = ocean_state.shape[1]
    chans = ocean_state.shape[2]
    forcing = jnp.dot(picked, w_couple, preferred_element_type=jnp.float32).reshape(
        grid_rows, grid_cols, chans
    )
    mask = land_mask.astype(jnp.float32)
    state = (mask[..., None] * (ocean_state.astype(jnp.float32) + forcing)).astype(jnp.bfloat16)
    count = dw_kernel.shape[0]
    for block in range(count):
        padded = with_halo(state, (("fsdp", 0), ("tile", 1)), 3)
        state = conv_block(
            padded, mask, dw_kernel[block], ocean_gain[block], w_pw1[block], w_pw2[block]
        )
    return (atm_out, state)


def solution(mesh):
    placed = (
        P("fsdp", "tile"),
        P(),
        P("fsdp", "tile"),
        P("tile", "fsdp"),
        P("tile", None),
        P(),
        P("fsdp", "tile", None),
        P("fsdp", "tile"),
        P("fsdp", "tile"),
        P(),
        P(),
        P(),
        P(),
        P(),
    )
    return jax.shard_map(
        body,
        mesh=mesh,
        in_specs=placed,
        out_specs=(P("fsdp", "tile"), P("fsdp", "tile", None)),
        check_vma=False,
    )
```

profile of v0, /device:TPU:7, one launch (start us, length us, event | category | flops | bytes accessed | tf_op | source)
XLA Modules:
  0.0 921.2 jit_solution(5960225791835715964)
XLA Ops:
  9.5 38.8 %all-gather.4.cloned.1.call-done = bf16[1024,1536]{1,0:T(8,128)(2,1)} async-done(((bf16[1024,384]{1,0:T(8,128)(2,1)}), bf16[1024,1536]{1,0:T(8,128)(2,1)}) %all-gather.4.cloned.1.call-update) | async-done | bytes 3145744 | tf_op jit(solution)/shard_map/all_gather | solution.py:64
  48.3 2.5 convert_reduce_fusion
  51.1 1.0 fusion.2
  52.1 237.8 %all-gather.6.cloned.1.call-done = bf16[1536,1536]{1,0:T(8,128)(2,1)} async-done(((bf16[24,1536]{1,0:T(8,128)(2,1)}), bf16[1536,1536]{1,0:T(8,128)(2,1)}) %all-gather.6.cloned.1.call-update) | async-done | bytes 4718608 | tf_op jit(solution)/shard_map/all_gather | solution.py:66
  289.9 304.7 %all-gather.8.cloned.1.call-done = bf16[1536,1536]{0,1:T(8,128)(2,1)} async-done(((bf16[1536,24]{0,1:T(8,128)(2,1)}), bf16[1536,1536]{0,1:T(8,128)(2,1)}) %all-gather.8.cloned.1.call-update) | async-done | bytes 4718608 | tf_op jit(solution)/shard_map/all_gather | solution.py:69
  594.6 17.4 %fusion.37 = f32[1024,1536]{1,0:T(8,128)} fusion(bf16[1536,1536]{0,1:T(8,128)(2,1)} %all-gather.8.cloned.1.call-done, bf16[1536,1536]{1,0:T(8,128)(2,1)} %all-gather.6.cloned.1.call-done, bf16[1024,1536]{1,0:T(8,128)(2,1)} %all-gather.4.cloned.1.call-done, f32[1536]{0:T(1024)S(1)} %copy-done.13, f32[1024]{0:T(1024)S(1)} %add_rsqrt_fusion.2, ...), kind=kOutput, calls=%fused_computation.44 | convolution fusion | flops 9685696512 | bytes 18888704 | tf_op jit(solution)/shard_map/dot_general | solution.py:70
  612.0 132.7 %reduce-scatter.2.cloned.1.call-done = f32[1024,384]{1,0:T(8,128)} async-done(((f32[1024,1536]{1,0:T(8,128)}), f32[1024,384]{1,0:T(8,128)}) %reduce-scatter.2.cloned.1.call-update) | async-done | bytes 1572880 | tf_op jit(solution)/shard_map/reduce_scatter | solution.py:71
  744.7 1.6 add_convert_fusion
  746.4 2.7 fusion.155
  749.5 80.5 %all-reduce.2.cloned.1.call-done = f32[1024,768]{1,0:T(8,128)} async-done(((f32[1024,768]{1,0:T(8,128)}), f32[1024,768]{1,0:T(8,128)}) %all-reduce.2.cloned.1.call-update) | async-done | bytes 3145744 | tf_op jit(solution)/shard_map/psum | solution.py:73
  830.0 3.0 fusion.58
  833.1 2.3 collective-permute-start
  835.5 6.3 collective-permute-start.1
  841.8 1.6 collective-permute-done.1
  843.4 3.2 gather_fusion
  847.3 2.0 collective-permute-start.2
  849.3 6.2 collective-permute-start.3
  855.6 1.1 collective-permute-done.3
  856.8 4.5 collective-permute-start.4
  861.4 1.9 collective-permute-start.5
  863.3 5.3 collective-permute-done.5
  869.1 9.1 fusion.142
  879.0 1.5 fusion.20
  881.2 1.9 collective-permute-start.6
  883.1 6.4 collective-permute-start.7
  889.6 1.1 collective-permute-done.7
  890.8 3.3 collective-permute-start.8
  894.1 2.1 collective-permute-start.9
  896.2 5.0 collective-permute-done.9
  901.8 9.1 fusion.140
  911.7 1.5 fusion.28
  913.1 1.5 fusion.57
  (80 shorter events, 7.0 us)
Async XLA Ops:
  7.2 739.2 %copy-start = (bf16[384,768]{1,0:T(8,128)(2,1)S(1)}, bf16[384,768]{1,0:T(8,128)(2,1)}, u32[]{:S(2)}) copy-start(bf16[384,768]{1,0:T(8,128)(2,1)} %param.18) | copy-start | bytes 1769476
  7.2 41.1 %all-gather.4.cloned.1.call-start = ((), (), s32[]{:S(2)}) async-start(), calls=%async_computation.1 | async-start | bytes 3932160 | tf_op jit(solution)/shard_map/all_gather | solution.py:64
  7.9 281.9 %all-gather.6.cloned.1.call-start = ((), (), s32[]{:S(2)}) async-start(), calls=%async_computation.2 | async-start | bytes 4792320 | tf_op jit(solution)/shard_map/all_gather | solution.py:66
  8.7 585.9 %all-gather.8.cloned.1.call-start = ((), (), s32[]{:S(2)}) async-start(), calls=%async_computation.3 | async-start | bytes 4792320 | tf_op jit(solution)/shard_map/all_gather | solution.py:69
  9.4 585.2 %copy-start.13 = (f32[1536]{0:T(1024)S(1)}, f32[1536]{0:T(1024)}, u32[]{:S(2)}) copy-start(f32[1536]{0:T(1024)} %param.15) | copy-start | bytes 18436
  9.4 735.3 %reduce-scatter.2.cloned.1.call-start = ((), (), s32[]{:S(2)}) async-start(), calls=%async_computation.4 | async-start | bytes 7864320 | tf_op jit(solution)/shard_map/reduce_scatter | solution.py:71
  48.3 2.8 copy-start.1
  612.0 132.7 %copy-start.2 = (bf16[1024,384]{1,0:T(8,128)(2,1)S(1)}, bf16[1024,384]{1,0:T(8,128)(2,1)}, u32[]{:S(2)}) copy-start(bf16[1024,384]{1,0:T(8,128)(2,1)} %param.14) | copy-start | bytes 2359300
  612.0 218.1 %all-reduce.2.cloned.1.call-start = ((), (), s32[]{:S(2)}) async-start(), calls=%async_computation.5 | async-start | bytes 6291456 | tf_op jit(solution)/shard_map/psum | solution.py:73
  746.3 2.8 copy-start.3
  746.3 2.8 copy-start.7
  746.3 2.9 copy-start.5
  746.4 83.7 %copy-start.12 = (bf16[768,128]{1,0:T(8,128)(2,1)S(1)}, bf16[768,128]{1,0:T(8,128)(2,1)}, u32[]{:S(2)}) copy-start(bf16[768,128]{1,0:T(8,128)(2,1)} %param.19) | copy-start | bytes 589828
  749.5 92.3 %copy-start.8 = (s32[32,32]{1,0:T(8,128)S(1)}, s32[32,32]{1,0:T(8,128)}, u32[]{:S(2)}) copy-start(s32[32,32]{1,0:T(8,128)} %param.21) | copy-start | bytes 12292
  833.1 13.6 %copy-start.6 = (bf16[128,256]{1,0:T(8,128)(2,1)S(1)}, bf16[128,256]{1,0:T(8,128)(2,1)}, u32[]{:S(2)}) copy-start(bf16[128,256]{1,0:T(8,128)(2,1)} %param.23) | copy-start | bytes 196612
  833.1 13.9 %copy-start.4 = (bf16[32,32,256]{2,1,0:T(8,128)(2,1)S(1)}, bf16[32,32,256]{2,1,0:T(8,128)(2,1)}, u32[]{:S(2)}) copy-start(bf16[32,32,256]{2,1,0:T(8,128)(2,1)} %param.20) | copy-start | bytes 1572868
  833.1 8.7 collective-permute-start
  835.5 7.9 collective-permute-start.1
  843.4 19.9 %copy-start.9 = (f32[2,256]{1,0:T(2,128)S(1)}, f32[2,256]{1,0:T(2,128)}, u32[]{:S(2)}) copy-start(f32[2,256]{1,0:T(2,128)} %param.25) | copy-start | bytes 6148
  847.3 8.3 collective-permute-start.2
  849.3 7.4 collective-permute-start.3
  856.8 6.5 collective-permute-start.4
  861.4 7.2 collective-permute-start.5
  869.1 9.9 %copy-start.10 = (bf16[2,256,1024]{2,1,0:T(8,128)(2,1)S(1)}, bf16[2,256,1024]{2,1,0:T(8,128)(2,1)}, u32[]{:S(2)}) copy-start(bf16[2,256,1024]{2,1,0:T(8,128)(2,1)} %param.26) | copy-start | bytes 3145732
  879.0 1.5 copy-start.11
  881.2 8.3 collective-permute-start.6
  883.1 7.5 collective-permute-start.7
  890.8 5.5 collective-permute-start.8
  894.1 7.2 collective-permute-start.9
Sparse Core Ops, SparseCore 0:
  9.8 38.4 all-gather.3
  50.1 239.7 all-gather.5
  291.7 302.8 all-gather.7
  612.1 132.5 reduce-scatter.1
  749.2 80.8 all-reduce.1
where the time goes:
time: 922 us; the launch traced here: 921 us
  waiting for transfers between devices  811 us (88%)
  starting transfers between devices  37.3 us (4%)
  matrix products  28.7 us (3%)
  other arithmetic  26.2 us (3%)
  between operations  14.3 us (2%)
    all_gather x1, waiting for transfers between devices, body(): down_whole = lax.all_gather(w_down, 'fsdp', axis=1, tiled=True)  305 us
    all_gather x1, waiting for transfers between devices, body(): up_whole = lax.all_gather(w_up, 'fsdp', axis=0, tiled=True)  238 us
    reduce_scatter x1, waiting for transfers between devices, body(): delta = lax.psum_scatter(terms, 'tile', scatter_dimension=1, tiled=True)  133 us
    psum x1, waiting for transfers between devices, body(): lax.psum(jnp.dot(atm_out, w_flux_in, preferred_element_type=jnp.float32),...  80.5 us
    all_gather x1, waiting for transfers between devices, body(): whole = lax.all_gather(tokens, 'tile', axis=1, tiled=True)  38.8 us
    ppermute x5, starting transfers between devices, with_halo(): lax.ppermute(lax.slice_in_dim(block, 0, width, axis=dim), axis, backward)  22.9 us
    reduce_sum x3, other arithmetic, layer_norm(): center = values - jnp.mean(values, axis=-1, keepdims=True)  20.7 us
  transfers between devices with their start and end apart: 15, of which 10 were waited for; matrix products, arithmetic and copies ran while one was open for 0% of the time, Pallas kernels for 0%

commit v1 on v0

--- a/solution.py
+++ b/solution.py
@@ -61,7 +61,9 @@
     w_pw2,
 ):
     band_rows = tokens.shape[0]
-    whole = lax.all_gather(tokens, "tile", axis=1, tiled=True)
+    whole = jnp.concatenate(
+        lax.all_to_all(jnp.stack([tokens] * lax.axis_size("tile")), "tile", 0, 0), axis=1
+    )
     normed = layer_norm(whole.astype(jnp.float32), ln_gain).astype(jnp.bfloat16)
     up_whole = lax.all_gather(w_up, "fsdp", axis=0, tiled=True)
     pre = jnp.dot(normed, up_whole, preferred_element_type=jnp.float32)

time: 922 us -> 887 us (0.962)
  waiting for transfers between devices: 811 us -> 713 us
  blocking collectives: 0 us -> 60.5 us
    all_to_all x0 -> x1, blocking collectives: none -> 60.5 us  [body(): lax.all_to_all(jnp.stack([tokens] * lax.axis_size('tile')), 'tile', 0, 0)]
    all_gather x1, waiting for transfers between devices: 238 us -> 180 us  [body(): up_whole = lax.all_gather(w_up, 'fsdp', axis=0, tiled=True)]
    all_gather x1 -> x0, waiting for transfers between devices: 38.8 us -> none  [body(): whole = lax.all_gather(tokens, 'tile', axis=1, tiled=True)]
  transfers between devices with their start and end apart: 15 -> 14, of which waited for: 10 -> 9; matrix products, arithmetic and copies ran while one was open for 0% -> 1% of each run, Pallas kernels for 0% -> 0%
where the time goes in v1:
time: 887 us
  waiting for transfers between devices  713 us (80%)
  blocking collectives  60.5 us (7%)
  starting transfers between devices  37.2 us (4%)
  matrix products  29.6 us (3%)
  other arithmetic  26.8 us (3%)
  between operations  14.3 us (2%)
    all_gather x1, waiting for transfers between devices, body(): down_whole = lax.all_gather(w_down, 'fsdp', axis=1, tiled=True)  304 us
    all_gather x1, waiting for transfers between devices, body(): up_whole = lax.all_gather(w_up, 'fsdp', axis=0, tiled=True)  180 us
    reduce_scatter x1, waiting for transfers between devices, body(): delta = lax.psum_scatter(terms, 'tile', scatter_dimension=1, tiled=True)  132 us
    psum x1, waiting for transfers between devices, body(): lax.psum(jnp.dot(atm_out, w_flux_in, preferred_element_type=jnp.float32),...  80.6 us
    all_to_all x1, blocking collectives, body(): lax.all_to_all(jnp.stack([tokens] * lax.axis_size('tile')), 'tile', 0, 0)  60.5 us
    ppermute x5, starting transfers between devices, with_halo(): lax.ppermute(lax.slice_in_dim(block, 0, width, axis=dim), axis, backward)  22.8 us
    reduce_sum x3, other arithmetic, layer_norm(): center = values - jnp.mean(values, axis=-1, keepdims=True)  18.8 us
    dot_general x1, matrix products, body(): terms = jnp.dot(hidden, down_whole, preferred_element_type=jnp.float32)  18.4 us
  transfers between devices with their start and end apart: 14, of which 9 were waited for; matrix products, arithmetic and copies ran while one was open for 1% of the time, Pallas kernels for 0%

profile of v1, /device:TPU:7, one launch (start us, length us, event | category | flops | bytes accessed | tf_op | source)
XLA Modules:
  0.0 886.6 jit_solution(5995068278365710750)
XLA Ops:
  8.7 1.4 copy.16
  10.5 60.5 %all_to_all.5 = bf16[4,1024,384]{1,2,0:T(8,128)(2,1)S(1)} all-to-all(bf16[4,1024,384]{1,2,0:T(8,128)(2,1)S(1)} %stack.2), channel_id=1, replica_groups=mesh['fsdp'=64,'tile'=4] {'tile'}, dimensions={0} | all-to-all | bytes 6291456 | tf_op jit(solution)/shard_map/all_to_all | solution.py:65
  72.6 2.6 fusion.10
  75.1 180.2 %all-gather.3.cloned.1.call-done = bf16[1536,1536]{1,0:T(8,128)(2,1)} async-done(((bf16[24,1536]{1,0:T(8,128)(2,1)}), bf16[1536,1536]{1,0:T(8,128)(2,1)}) %all-gather.3.cloned.1.call-update) | async-done | bytes 4718608 | tf_op jit(solution)/shard_map/all_gather | solution.py:68
  255.3 303.7 %all-gather.5.cloned.1.call-done = bf16[1536,1536]{0,1:T(8,128)(2,1)} async-done(((bf16[1536,24]{0,1:T(8,128)(2,1)}), bf16[1536,1536]{0,1:T(8,128)(2,1)}) %all-gather.5.cloned.1.call-update) | async-done | bytes 4718608 | tf_op jit(solution)/shard_map/all_gather | solution.py:71
  559.0 18.4 %fusion.35 = f32[1024,1536]{1,0:T(8,128)} fusion(bf16[1536,1536]{0,1:T(8,128)(2,1)} %all-gather.5.cloned.1.call-done, bf16[1024,1536]{0,1:T(8,128)(2,1)} %fusion.10, bf16[1536,1536]{1,0:T(8,128)(2,1)} %all-gather.3.cloned.1.call-done), kind=kOutput, calls=%fused_computation.42 | convolution fusion | flops 9677832192 | bytes 18874368 | tf_op jit(solution)/shard_map/dot_general | solution.py:72
  577.6 132.5 %reduce-scatter.2.cloned.1.call-done = f32[1024,384]{1,0:T(8,128)} async-done(((f32[1024,1536]{1,0:T(8,128)}), f32[1024,384]{1,0:T(8,128)}) %reduce-scatter.2.cloned.1.call-update) | async-done | bytes 1572880 | tf_op jit(solution)/shard_map/reduce_scatter | solution.py:73
  710.1 1.6 add_convert_fusion
  711.8 2.7 fusion.146
  714.9 80.6 %all-reduce.2.cloned.1.call-done = f32[1024,768]{1,0:T(8,128)} async-done(((f32[1024,768]{1,0:T(8,128)}), f32[1024,768]{1,0:T(8,128)}) %all-reduce.2.cloned.1.call-update) | async-done | bytes 3145744 | tf_op jit(solution)/shard_map/psum | solution.py:75
  795.5 3.0 fusion.47
  798.5 2.3 collective-permute-start
  800.9 6.1 collective-permute-start.1
  807.0 1.8 collective-permute-done.1
  808.9 3.2 gather_fusion
  812.7 2.0 collective-permute-start.2
  814.8 6.2 collective-permute-start.3
  821.1 1.1 collective-permute-done.3
  822.3 4.5 collective-permute-start.4
  826.8 1.9 collective-permute-start.5
  828.7 5.3 collective-permute-done.5
  834.5 9.1 %fusion.131 = (f32[32,32]{1,0:T(8,128)S(1)}, f32[32,32,256]{2,1,0:T(8,128)S(1)}) fusion(f32[256]{0:T(256)S(1)} %bitcast.188, bf16[38,35,256]{2,1,0:T(8,128)(2,1)S(1)} %get-tuple-element.11, f32[256]{0:T(256)S(1)} %bitcast.189, f32[256]{0:T(256)S(1)} %bitcast.190, f32[256]{0:T(256)S(1)} %bitcast.191, bf16[3,32,256]{2,1,0:T(8,128)(2,1)S(1)} %collective-permute-done.3, ...), kind=kLoop, calls=%fused_computation.188 | loop fusion | flops 40107008 | bytes 23745536 | tf_op jit(solution)/shard_map/reduce_sum | solution.py:21
  844.4 1.5 fusion.18
  846.7 1.9 collective-permute-start.6
  848.6 6.4 collective-permute-start.7
  855.0 1.1 collective-permute-done.7
  856.2 3.3 collective-permute-start.8
  859.5 2.1 collective-permute-start.9
  861.7 5.0 collective-permute-done.9
  867.2 9.1 %fusion.129 = (f32[32,32]{1,0:T(8,128)S(1)}, f32[32,32,256]{2,1,0:T(8,128)S(1)}) fusion(f32[256]{0:T(256)S(1)} %bitcast.150, bf16[38,35,256]{2,1,0:T(8,128)(2,1)S(1)} %get-tuple-element.7, f32[256]{0:T(256)S(1)} %bitcast.151, f32[256]{0:T(256)S(1)} %bitcast.152, f32[256]{0:T(256)S(1)} %bitcast.153, bf16[3,32,256]{2,1,0:T(8,128)(2,1)S(1)} %collective-permute-done.7, ...), kind=kLoop, calls=%fused_computation.187 | loop fusion | flops 40107008 | bytes 23745536 | tf_op jit(solution)/shard_map/reduce_sum | solution.py:21
  877.1 1.5 fusion.26
  878.6 1.5 fusion.46
  (79 shorter events, 8.1 us)
Async XLA Ops:
  7.2 704.6 %copy-start = (bf16[384,768]{1,0:T(8,128)(2,1)S(1)}, bf16[384,768]{1,0:T(8,128)(2,1)}, u32[]{:S(2)}) copy-start(bf16[384,768]{1,0:T(8,128)(2,1)} %param.18) | copy-start | bytes 1769476
  7.2 248.1 %all-gather.3.cloned.1.call-start = ((), (), s32[]{:S(2)}) async-start(), calls=%async_computation.2 | async-start | bytes 4792320 | tf_op jit(solution)/shard_map/all_gather | solution.py:68
  7.9 551.1 %all-gather.5.cloned.1.call-start = ((), (), s32[]{:S(2)}) async-start(), calls=%async_computation.3 | async-start | bytes 4792320 | tf_op jit(solution)/shard_map/all_gather | solution.py:71
  8.7 701.5 %reduce-scatter.2.cloned.1.call-start = ((), (), s32[]{:S(2)}) async-start(), calls=%async_computation.4 | async-start | bytes 7864320 | tf_op jit(solution)/shard_map/reduce_scatter | solution.py:73
  71.0 1.5 copy-start.8
  577.4 132.7 %copy-start.1 = (bf16[1024,384]{1,0:T(8,128)(2,1)S(1)}, bf16[1024,384]{1,0:T(8,128)(2,1)}, u32[]{:S(2)}) copy-start(bf16[1024,384]{1,0:T(8,128)(2,1)} %param.14) | copy-start | bytes 2359300
  577.4 218.1 %all-reduce.2.cloned.1.call-start = ((), (), s32[]{:S(2)}) async-start(), calls=%async_computation.5 | async-start | bytes 6291456 | tf_op jit(solution)/shard_map/psum | solution.py:75
  711.7 2.7 copy-start.2
  711.8 2.7 copy-start.6
  711.8 2.9 copy-start.4
  711.8 83.7 %copy-start.12 = (bf16[768,128]{1,0:T(8,128)(2,1)S(1)}, bf16[768,128]{1,0:T(8,128)(2,1)}, u32[]{:S(2)}) copy-start(bf16[768,128]{1,0:T(8,128)(2,1)} %param.19) | copy-start | bytes 589828
  714.9 92.1 %copy-start.7 = (s32[32,32]{1,0:T(8,128)S(1)}, s32[32,32]{1,0:T(8,128)}, u32[]{:S(2)}) copy-start(s32[32,32]{1,0:T(8,128)} %param.21) | copy-start | bytes 12292
  798.5 13.6 %copy-start.5 = (bf16[128,256]{1,0:T(8,128)(2,1)S(1)}, bf16[128,256]{1,0:T(8,128)(2,1)}, u32[]{:S(2)}) copy-start(bf16[128,256]{1,0:T(8,128)(2,1)} %param.23) | copy-start | bytes 196612
  798.5 13.9 %copy-start.3 = (bf16[32,32,256]{2,1,0:T(8,128)(2,1)S(1)}, bf16[32,32,256]{2,1,0:T(8,128)(2,1)}, u32[]{:S(2)}) copy-start(bf16[32,32,256]{2,1,0:T(8,128)(2,1)} %param.20) | copy-start | bytes 1572868
  798.5 8.5 collective-permute-start
  800.9 7.9 collective-permute-start.1
  808.8 19.9 %copy-start.9 = (f32[2,256]{1,0:T(2,128)S(1)}, f32[2,256]{1,0:T(2,128)}, u32[]{:S(2)}) copy-start(f32[2,256]{1,0:T(2,128)} %param.25) | copy-start | bytes 6148
  812.7 8.3 collective-permute-start.2
  814.8 7.4 collective-permute-start.3
  822.3 6.5 collective-permute-start.4
  826.8 7.2 collective-permute-start.5
  834.5 9.9 %copy-start.10 = (bf16[2,256,1024]{2,1,0:T(8,128)(2,1)S(1)}, bf16[2,256,1024]{2,1,0:T(8,128)(2,1)}, u32[]{:S(2)}) copy-start(bf16[2,256,1024]{2,1,0:T(8,128)(2,1)} %param.26) | copy-start | bytes 3145732
  844.4 1.5 copy-start.11
  846.7 8.3 collective-permute-start.6
  848.6 7.5 collective-permute-start.7
  856.2 5.5 collective-permute-start.8
  859.5 7.2 collective-permute-start.9
Sparse Core Ops, SparseCore 0:
  9.8 245.4 all-gather.2
  257.1 301.8 all-gather.4
  577.5 132.5 reduce-scatter.1
  714.6 80.8 all-reduce.1
